TPU v7x, 32 devices: a whole 2x2x4 slice. The times are simulated.
32 devices in a mesh: groups: 2 (over x), seq: 16 (over z, y, core).
Axes of the slice: x: 2, y: 2, z: 4, core: 2. Of those that a mesh axis runs over, the one named last changes fastest.
Arguments:
- inputs: bfloat16 [16384, 768], P(('groups', 'seq')), parts along dimension 0, may hold values from -6 to 6
- gates: bfloat16 [16384, 768], P(('groups', 'seq')), parts along dimension 0, may hold values from -6 to 6
- cotangent: bfloat16 [16384, 768], P(('groups', 'seq')), parts along dimension 0, may hold values from -6 to 6
- first_factor: bfloat16 [16, 512, 512], P('seq'), may hold values from -0.25 to 0.25
- second_factor: bfloat16 [512, 16, 16], P('seq'), may hold values from -1.5 to 1.5
- channel_gain: float32 [768], replicated, may hold values from 0.1 to 1.9
Outputs:
- layer_output: bfloat16 [16384, 768], P(('groups', 'seq')), parts along dimension 0
- grad_inputs: bfloat16 [16384, 768], P(('groups', 'seq')), parts along dimension 0
- grad_gates: bfloat16 [16384, 768], P(('groups', 'seq')), parts along dimension 0
- grad_first: bfloat16 [32, 512, 512], P(('groups', 'seq')), parts along dimension 0
- grad_second: bfloat16 [1024, 16, 16], P(('groups', 'seq')), parts along dimension 0
- gain_grad: float32 [1536], P('groups'), parts along dimension 0
There are 2 independent parts, one for each index of `groups`. A program takes and returns all parts, laid end to end along the dimension named above; an argument that names none is the same for every part. Nothing has to cross between parts.
All inputs are finite; a program needn't handle non-finite values.
Results may differ from a plain program's by a relative error of at most 0.0085.
Values may be sent and summed in bfloat16 or wider, within the bound.
A program may use at most 64 MiB of HBM per device.

v0:
```python
import math

import jax
import jax.numpy as jnp
from jax import lax
from jax.sharding import PartitionSpec as P


def lower_mask(extent):
    row_ids = lax.broadcasted_iota(jnp.int32, (extent, extent), 0)
    col_ids = lax.broadcasted_iota(jnp.int32, (extent, extent), 1)
    return col_ids <= row_ids


def on_device(inputs, gates, cotangent, first_factor, second_factor, channel_gain):
    block_count = first_factor.shape[0]
    block_size = first_factor.shape[1]
    channels = inputs.shape[1]
    block_total = second_factor.shape[1]
    rows3 = inputs.reshape(block_count, block_size, channels)
    gates3 = gates.reshape(block_count, block_size, channels)
    upstream3 = cotangent.reshape(block_count, block_size, channels)
    mask_first = lower_mask(block_size)
    mask_second = lower_mask(block_total)
    first_masked = jnp.where(mask_first[None], first_factor, jnp.zeros((), first_factor.dtype))
    second_masked = jnp.where(mask_second[None], second_factor, jnp.zeros((), second_factor.dtype))
    norm_factor = 1.0 / math.sqrt(inputs.shape[0] * lax.axis_size("seq"))
    gates_cols, upstream_cols = (
        lax.all_to_all(gates3, "seq", split_axis=1, concat_axis=0, tiled=True),
        lax.all_to_all(upstream3, "seq", split_axis=1, concat_axis=0, tiled=True),
    )
    first_mixed = jnp.einsum(
        "kab,kbc->kac", first_masked, rows3, preferred_element_type=jnp.float32
    ).astype(jnp.bfloat16)
    columns = lax.all_to_all(first_mixed, "seq", split_axis=1, concat_axis=0, tiled=True)
    second_cols = jnp.einsum(
        "jab,bjc->ajc", second_masked, columns, preferred_element_type=jnp.float32
    ).astype(jnp.bfloat16)
    hidden_values = second_cols.astype(jnp.float32)
    gate_values = gates_cols.astype(jnp.float32)
    upstream_values = upstream_cols.astype(jnp.float32)
    output_cols = (gate_values * channel_gain * hidden_values).astype(jnp.bfloat16)
    hidden_cols = (upstream_values * gate_values * channel_gain).astype(jnp.bfloat16)
    grad_gate_cols = (upstream_values * channel_gain * hidden_values).astype(jnp.bfloat16)
    partial_gain = jnp.sum(upstream_values * gate_values * hidden_values, axis=(0, 1))
    grad_pairs = jnp.einsum(
        "ajc,bjc->jab", hidden_cols, columns, preferred_element_type=jnp.float32
    )
    grad_sec = jnp.where(mask_second[None], grad_pairs, jnp.zeros((), jnp.float32)).astype(
        jnp.bfloat16
    )
    back_cols = jnp.einsum(
        "jab,ajc->bjc", second_masked, hidden_cols, preferred_element_type=jnp.float32
    ).astype(jnp.bfloat16)
    back_rows, output_rows, grad_gate_rows = (
        lax.all_to_all(back_cols, "seq", split_axis=0, concat_axis=1, tiled=True),
        lax.all_to_all(output_cols, "seq", split_axis=0, concat_axis=1, tiled=True),
        lax.all_to_all(grad_gate_cols, "seq", split_axis=0, concat_axis=1, tiled=True),
    )
    gain_grad = lax.psum(partial_gain, "seq") * norm_factor
    grad_pairs_first = jnp.einsum(
        "kac,kbc->kab", back_rows, rows3, preferred_element_type=jnp.float32
    )
    grad_first = jnp.where(mask_first[None], grad_pairs_first, jnp.zeros((), jnp.float32)).astype(
        jnp.bfloat16
    )
    grad_in = jnp.einsum(
        "kab,kac->kbc", first_masked, back_rows, preferred_element_type=jnp.float32
    ).astype(jnp.bfloat16)
    token_rows = inputs.shape[0]
    return (
        output_rows.reshape(token_rows, channels),
        grad_in.reshape(token_rows, channels),
        grad_gate_rows.reshape(token_rows, channels),
        grad_first,
        grad_sec,
        gain_grad,
    )


def solution(mesh):
    placed = (
        P(("groups", "seq"), None),
        P(("groups", "seq"), None),
        P(("groups", "seq"), None),
        P("seq", None, None),
        P("seq", None, None),
        P(),
    )
    return jax.shard_map(
        on_device,
        mesh=mesh,
        in_specs=placed,
        out_specs=(
            P(("groups", "seq"), None),
            P(("groups", "seq"), None),
            P(("groups", "seq"), None),
            P(("groups", "seq"), None, None),
            P(("groups", "seq"), None, None),
            P("groups"),
        ),
        check_vma=False,
    )
```

profile of v0, /device:TPU:0, one launch (start us, length us, event | category | flops | bytes accessed | tf_op | source)
XLA Modules:
  0.0 196.3 jit_solution(10928412952804270693)
XLA Ops:
  0.6 0.0 copy-start
  0.6 1.1 copy-done
  1.8 1.6 fusion.5
  3.4 1.2 copy.83
  4.6 0.5 broadcast.2
  5.1 5.4 %reduce.2 = bf16[512,768]{1,0:T(8,128)(2,1)S(1)} reduce(bf16[512,1,768]{2,1,0:T(2,128)(2,1)S(1)} %bitcast.48, bf16[]{:T(256)} %broadcast.2), dimensions={1}, to_apply=%bitcast.46.reduce_sub_computation | reduce | bytes 1572866
  10.6 1.1 reshape.99
  11.6 0.0 copy-start.4
  11.6 7.6 %all-to-all-start.1 = ((bf16[16,2,12288]{2,1,0:T(2,128)(2,1)}), bf16[16,2,12288]{2,1,0:T(2,128)(2,1)}, u32[]{:S(2)}, u32[]{:S(2)}) async-start(bf16[16,2,12288]{2,1,0:T(2,128)(2,1)} %reshape.99), calls=%async_computation.1 | async-start | bytes 1572864 | tf_op jit(solution)/shard_map/all_to_all | solution.py:35
  19.2 0.0 copy-done.4
  19.2 1.2 copy.84
  20.4 5.4 %reduce = bf16[512,768]{1,0:T(8,128)(2,1)S(1)} reduce(bf16[512,1,768]{2,1,0:T(2,128)(2,1)S(1)} %bitcast.53, bf16[]{:T(256)} %broadcast.2), dimensions={1}, to_apply=%bitcast.47.reduce_sub_computation | reduce | bytes 1572866
  25.9 1.1 reshape.101
  26.9 0.0 copy-start.5
  26.9 11.0 %all-to-all-done.1 = bf16[16,2,12288]{2,1,0:T(2,128)(2,1)} async-done(((bf16[16,2,12288]{2,1,0:T(2,128)(2,1)}), bf16[16,2,12288]{2,1,0:T(2,128)(2,1)}, u32[]{:S(2)}, u32[]{:S(2)}) %all-to-all-start.1) | async-done | bytes 786464 | tf_op jit(solution)/shard_map/all_to_all | solution.py:35
  38.0 5.5 %all-to-all-start = ((bf16[16,2,12288]{2,1,0:T(2,128)(2,1)}), bf16[16,2,12288]{2,1,0:T(2,128)(2,1)}, u32[]{:S(2)}, u32[]{:S(2)}) async-start(bf16[16,2,12288]{2,1,0:T(2,128)(2,1)} %reshape.101), calls=%async_computation | async-start | bytes 1572864 | tf_op jit(solution)/shard_map/all_to_all | solution.py:29
  43.5 0.0 copy-done.5
  43.5 1.2 copy.82
  44.7 5.4 %reduce.1 = bf16[512,768]{1,0:T(8,128)(2,1)S(1)} reduce(bf16[512,1,768]{2,1,0:T(2,128)(2,1)S(1)} %bitcast.49, bf16[]{:T(256)} %broadcast.2), dimensions={1}, to_apply=%bitcast.45.reduce_sub_computation | reduce | bytes 1572866
  50.2 0.0 copy-start.6
  50.2 1.1 reshape.103
  51.2 11.0 %all-to-all-done = bf16[16,2,12288]{2,1,0:T(2,128)(2,1)} async-done(((bf16[16,2,12288]{2,1,0:T(2,128)(2,1)}), bf16[16,2,12288]{2,1,0:T(2,128)(2,1)}, u32[]{:S(2)}, u32[]{:S(2)}) %all-to-all-start) | async-done | bytes 786464 | tf_op jit(solution)/shard_map/all_to_all | solution.py:29
  62.3 5.5 %all-to-all-start.3 = ((bf16[16,2,12288]{2,1,0:T(2,128)(2,1)}), bf16[16,2,12288]{2,1,0:T(2,128)(2,1)S(1)}, u32[]{:S(2)}, u32[]{:S(2)}) async-start(bf16[16,2,12288]{2,1,0:T(2,128)(2,1)} %reshape.103), calls=%async_computation.3 | async-start | bytes 1572864 | tf_op jit(solution)/shard_map/all_to_all | solution.py:30
  67.7 0.0 copy-done.6
  67.8 0.2 copy.46
  67.9 4.4 %reshape.100 = bf16[512,1,768]{2,1,0:T(2,128)(2,1)S(1)} reshape(bf16[16,2,12288]{2,1,0:T(2,128)(2,1)} %all-to-all-done.1) | data formatting | bytes 1572864
  72.3 1.0 copy.60
  73.3 4.4 %reshape.102 = bf16[512,1,768]{2,1,0:T(2,128)(2,1)S(1)} reshape(bf16[16,2,12288]{2,1,0:T(2,128)(2,1)} %all-to-all-done) | data formatting | bytes 1572864
  77.7 0.1 copy.43
  77.8 1.3 convert.3
  79.1 7.3 %all-to-all-done.3 = bf16[16,2,12288]{2,1,0:T(2,128)(2,1)S(1)} async-done(((bf16[16,2,12288]{2,1,0:T(2,128)(2,1)}), bf16[16,2,12288]{2,1,0:T(2,128)(2,1)S(1)}, u32[]{:S(2)}, u32[]{:S(2)}) %all-to-all-start.3) | async-done | bytes 786464 | tf_op jit(solution)/shard_map/all_to_all | solution.py:30
  86.4 0.7 reshape.104
  87.2 0.0 copy-start.7
  87.2 0.1 copy.50
  87.3 0.0 copy-start.1
  87.3 0.0 copy-start.2
  87.4 0.2 convert.4
  87.5 0.4 copy-done.7
  87.9 0.8 copy-done.1
  88.7 0.2 copy-done.2
  88.9 2.4 %fusion.2 = (f32[768]{0:T(1024)S(1)}, bf16[16,32,768]{2,0,1:T(8,128)(2,1)S(1)}, bf16[16,32,768]{2,0,1:T(8,128)(2,1)S(1)}, bf16[16,32,768]{2,0,1:T(8,128)(2,1)S(1)}) fusion(f32[16,32,768]{2,1,0:T(8,128)S(1)} %copy-done.1, f32[16,32,768]{2,1,0:T(8,128)S(1)} %convert.4, f32[768]{0:T(1024)S(1)} %copy-done.7, bf16[16,32,768]{2,1,0:T(8,128)(2,1)S(1)} %bitcast.58, ...), kind=kOutput, calls=%fused_computation.5 | convolution fusion | flops 17702144 | bytes 6314240 | tf_op jit(solution)/shard_map/jab,bjc->ajc/dot_general | solution.py:36
  91.4 0.0 copy-start.3
  91.4 0.9 copy-done.3
  92.3 0.4 fusion.4
  92.7 1.1 copy.54
  93.8 5.5 %all-to-all-start.4 = ((bf16[16,32,768]{2,1,0:T(8,128)(2,1)}), bf16[16,32,768]{2,1,0:T(8,128)(2,1)}, u32[]{:S(2)}, u32[]{:S(2)}) async-start(bf16[16,32,768]{2,1,0:T(8,128)(2,1)} %copy.54), calls=%async_computation.4 | async-start | bytes 1572864 | tf_op jit(solution)/shard_map/all_to_all | solution.py:56
  99.3 1.1 copy.56
  100.5 17.7 %all-to-all-done.4 = bf16[16,32,768]{2,1,0:T(8,128)(2,1)} async-done(((bf16[16,32,768]{2,1,0:T(8,128)(2,1)}), bf16[16,32,768]{2,1,0:T(8,128)(2,1)}, u32[]{:S(2)}, u32[]{:S(2)}) %all-to-all-start.4) | async-done | bytes 786464 | tf_op jit(solution)/shard_map/all_to_all | solution.py:56
  118.1 5.5 %all-to-all-start.5 = ((bf16[16,32,768]{2,1,0:T(8,128)(2,1)}), bf16[16,32,768]{2,1,0:T(8,128)(2,1)S(1)}, u32[]{:S(2)}, u32[]{:S(2)}) async-start(bf16[16,32,768]{2,1,0:T(8,128)(2,1)} %copy.56), calls=%async_computation.5 | async-start | bytes 1572864 | tf_op jit(solution)/shard_map/all_to_all | solution.py:58
  123.6 1.1 copy.48
  124.7 17.6 %all-to-all-done.5 = bf16[16,32,768]{2,1,0:T(8,128)(2,1)S(1)} async-done(((bf16[16,32,768]{2,1,0:T(8,128)(2,1)}), bf16[16,32,768]{2,1,0:T(8,128)(2,1)S(1)}, u32[]{:S(2)}, u32[]{:S(2)}) %all-to-all-start.5) | async-done | bytes 786464 | tf_op jit(solution)/shard_map/all_to_all | solution.py:58
  142.3 5.5 %all-to-all-start.2 = ((bf16[16,32,768]{2,1,0:T(8,128)(2,1)}), bf16[16,32,768]{2,1,0:T(8,128)(2,1)S(1)}, u32[]{:S(2)}, u32[]{:S(2)}) async-start(bf16[16,32,768]{2,1,0:T(8,128)(2,1)} %copy.48), calls=%async_computation.2 | async-start | bytes 1572864 | tf_op jit(solution)/shard_map/all_to_all | solution.py:57
  147.8 1.7 fusion.7
  149.5 0.0 copy-start.8
  149.5 0.8 copy.58
  150.3 38.5 %psum.7 = f32[768]{0:T(1024)S(1)} all-reduce(f32[768]{0:T(1024)S(1)} %get-tuple-element.30), channel_id=1, replica_groups=mesh['groups'=2,'seq'=16] {'seq'}, use_global_device_ids=true, to_apply=%region_1.2 | all-reduce | flops 768 | bytes 6144 | tf_op jit(solution)/shard_map/psum | solution.py:60
  188.8 0.6 broadcast_multiply_fusion
  189.4 2.5 %fusion.6 = bf16[1,512,512]{2,1,0:T(8,128)(2,1)} fusion(bf16[512,768]{1,0:T(8,128)(2,1)} %bitcast.10, bf16[512,768]{1,0:T(8,128)(2,1)S(1)} %copy-done), kind=kOutput, calls=%fused_computation.16 | convolution fusion | flops 403439616 | bytes 2097152 | tf_op jit(solution)/shard_map/kac,kbc->kab/dot_general | solution.py:61
  191.9 0.0 copy-done.8
  191.9 2.6 %convolution_convert_fusion = bf16[512,768]{1,0:T(8,128)(2,1)} fusion(bf16[512,768]{1,0:T(8,128)(2,1)} %bitcast.10, bf16[1,512,512]{2,1,0:T(8,128)(2,1)S(1)} %copy-done.8), kind=kOutput, calls=%fused_computation.8 | convolution fusion | flops 403570688 | bytes 2097152 | tf_op jit(solution)/shard_map/kab,kac->kbc/dot_general | solution.py:67
  194.5 0.0 all-to-all-done.2
  194.5 0.9 copy.87
  195.4 0.9 copy.88
  (1 shorter events, 0.0 us)
Async XLA Ops:
  0.6 1.1 copy-start
  11.6 7.6 %copy-start.4 = (bf16[512,768]{1,0:T(8,128)(2,1)S(1)}, bf16[512,768]{1,0:T(8,128)(2,1)}, u32[]{:S(2)}) copy-start(bf16[512,768]{1,0:T(8,128)(2,1)} %param.7) | copy-start | bytes 2359300
  11.6 26.3 %all-to-all-start.1 = ((bf16[16,2,12288]{2,1,0:T(2,128)(2,1)}), bf16[16,2,12288]{2,1,0:T(2,128)(2,1)}, u32[]{:S(2)}, u32[]{:S(2)}) async-start(bf16[16,2,12288]{2,1,0:T(2,128)(2,1)} %reshape.99), calls=%async_computation.1 | async-start | bytes 1572864 | tf_op jit(solution)/shard_map/all_to_all | solution.py:35
  26.9 16.6 %copy-start.5 = (bf16[512,768]{1,0:T(8,128)(2,1)S(1)}, bf16[512,768]{1,0:T(8,128)(2,1)}, u32[]{:S(2)}) copy-start(bf16[512,768]{1,0:T(8,128)(2,1)} %param.8) | copy-start | bytes 2359300
  38.0 24.3 %all-to-all-start = ((bf16[16,2,12288]{2,1,0:T(2,128)(2,1)}), bf16[16,2,12288]{2,1,0:T(2,128)(2,1)}, u32[]{:S(2)}, u32[]{:S(2)}) async-start(bf16[16,2,12288]{2,1,0:T(2,128)(2,1)} %reshape.101), calls=%async_computation | async-start | bytes 1572864 | tf_op jit(solution)/shard_map/all_to_all | solution.py:29
  50.2 17.6 %copy-start.6 = (bf16[32,16,16]{0,2,1:T(8,128)(2,1)S(1)}, bf16[32,16,16]{0,2,1:T(8,128)(2,1)}, u32[]{:S(2)}) copy-start(bf16[32,16,16]{0,2,1:T(8,128)(2,1)} %param.10) | copy-start | bytes 49156
  62.3 24.2 %all-to-all-start.3 = ((bf16[16,2,12288]{2,1,0:T(2,128)(2,1)}), bf16[16,2,12288]{2,1,0:T(2,128)(2,1)S(1)}, u32[]{:S(2)}, u32[]{:S(2)}) async-start(bf16[16,2,12288]{2,1,0:T(2,128)(2,1)} %reshape.103), calls=%async_computation.3 | async-start | bytes 1572864 | tf_op jit(solution)/shard_map/all_to_all | solution.py:30
  87.2 0.7 copy-start.7
  87.3 1.4 copy-start.1
  87.3 1.6 copy-start.2
  91.4 0.9 copy-start.3
  93.8 24.3 %all-to-all-start.4 = ((bf16[16,32,768]{2,1,0:T(8,128)(2,1)}), bf16[16,32,768]{2,1,0:T(8,128)(2,1)}, u32[]{:S(2)}, u32[]{:S(2)}) async-start(bf16[16,32,768]{2,1,0:T(8,128)(2,1)} %copy.54), calls=%async_computation.4 | async-start | bytes 1572864 | tf_op jit(solution)/shard_map/all_to_all | solution.py:56
  118.1 24.2 %all-to-all-start.5 = ((bf16[16,32,768]{2,1,0:T(8,128)(2,1)}), bf16[16,32,768]{2,1,0:T(8,128)(2,1)S(1)}, u32[]{:S(2)}, u32[]{:S(2)}) async-start(bf16[16,32,768]{2,1,0:T(8,128)(2,1)} %copy.56), calls=%async_computation.5 | async-start | bytes 1572864 | tf_op jit(solution)/shard_map/all_to_all | solution.py:58
  142.3 52.2 %all-to-all-start.2 = ((bf16[16,32,768]{2,1,0:T(8,128)(2,1)}), bf16[16,32,768]{2,1,0:T(8,128)(2,1)S(1)}, u32[]{:S(2)}, u32[]{:S(2)}) async-start(bf16[16,32,768]{2,1,0:T(8,128)(2,1)} %copy.48), calls=%async_computation.2 | async-start | bytes 1572864 | tf_op jit(solution)/shard_map/all_to_all | solution.py:57
  149.5 42.4 %copy-start.8 = (bf16[1,512,512]{2,1,0:T(8,128)(2,1)S(1)}, bf16[1,512,512]{2,1,0:T(8,128)(2,1)}, u32[]{:S(2)}) copy-start(bf16[1,512,512]{2,1,0:T(8,128)(2,1)} %param.9) | copy-start | bytes 1572868
where the time goes:
time: 197 us; the launch traced here: 196 us
  waiting for transfers between devices  64.6 us (33%)
  blocking collectives  38.5 us (20%)
  starting transfers between devices  35.1 us (18%)
  local copies, waits for them, and re-layouts  27.5 us (14%)
  other arithmetic  18.3 us (9%)
  matrix products  11.3 us (6%)
    psum x1, blocking collectives, on_device(): gain_grad = lax.psum(partial_gain, 'seq') * norm_factor  38.5 us
    unnamed x30, local copies, waits for them, and re-layouts  20.3 us
    all_to_all x1, waiting for transfers between devices, on_device(): lax.all_to_all(back_cols, 'seq', split_axis=0, concat_axis=1, tiled=True)  17.7 us
    all_to_all x1, waiting for transfers between devices, on_device(): lax.all_to_all(grad_gate_cols, 'seq', split_axis=0, concat_axis=1, tiled=...  17.6 us
    unnamed x3, other arithmetic  16.3 us
    all_to_all x1, waiting for transfers between devices, on_device(): lax.all_to_all(first_mixed, 'seq', split_axis=1, concat_axis=0, tiled=True)  11 us
    all_to_all x1, waiting for transfers between devices, on_device(): lax.all_to_all(gates3, 'seq', split_axis=1, concat_axis=0, tiled=True)  11 us
    all_to_all x1, starting transfers between devices, on_device(): lax.all_to_all(first_mixed, 'seq', split_axis=1, concat_axis=0, tiled=True)  7.57 us
  transfers between devices with their start and end apart: 6, of which 5 were waited for; matrix products, arithmetic and copies ran while one was open for 19% of the time, Pallas kernels for 0%

commit v1 on v0

v1 whole, which is shorter than its diff:
```python
import functools
import math

import jax
import jax.numpy as jnp
from jax import lax
from jax.experimental import pallas as pl
from jax.experimental.pallas import tpu as pltpu
from jax.sharding import PartitionSpec as P

BF16 = jnp.bfloat16
F32 = jnp.float32


def lower_mask(extent):
    row_ids = lax.broadcasted_iota(jnp.int32, (extent, extent), 0)
    col_ids = lax.broadcasted_iota(jnp.int32, (extent, extent), 1)
    return col_ids <= row_ids


def dot(a, b, ca=1, cb=0):
    return lax.dot_general(a, b, (((ca,), (cb,)), ((), ())), preferred_element_type=F32)


def fused_kernel(
    n, x_ref, g_ref, u_ref, f_ref, s_ref, gain_ref,
    out_ref, gin_ref, ggate_ref, gfirst_ref, gsec_ref, ggain_ref,
    f_masked, weights, gh_rows, fm_rows, gh_cols, fm_cols, back_cols, sec_cols, back_rows, sec_rows,
    gain_all, send, recv,
):
    block, channels = x_ref.shape
    jpd = block // n
    me = lax.axis_index("seq")
    barrier = pltpu.get_barrier_semaphore()

    @pl.loop(1, n)
    def _(k):
        pl.semaphore_signal(
            barrier, inc=1, device_id={"seq": lax.rem(me + k, n)}, device_id_type=pl.DeviceIdType.MESH
        )

    def copy_to(phase, src, dst, peer, src_slot):
        return pltpu.make_async_remote_copy(
            src_ref=src.at[src_slot],
            dst_ref=dst.at[me],
            send_sem=send.at[phase, peer],
            recv_sem=recv.at[phase, me],
            device_id={"seq": peer},
            device_id_type=pl.DeviceIdType.MESH,
        )

    def copy_from(phase, src, dst, peer, src_slot):
        return pltpu.make_async_remote_copy(
            src_ref=src.at[src_slot],
            dst_ref=dst.at[peer],
            send_sem=send.at[phase, peer],
            recv_sem=recv.at[phase, peer],
            device_id={"seq": peer},
            device_id_type=pl.DeviceIdType.MESH,
        )

    def start_all(phase, src, dst):
        @pl.loop(1, n)
        def _(k):
            peer = lax.rem(me + k, n)
            copy_to(phase, src, dst, peer, peer).start()

    def wait_all(phase, src, dst):
        @pl.loop(1, n)
        def _(k):
            peer = lax.rem(me + k, n)
            copy_from(phase, src, dst, peer, peer).wait_recv()

    gain = gain_ref[...]
    rows = lambda ref: ref[...].reshape(block, channels)
    split = lambda value: value.reshape(n, jpd, channels)

    gh_rows[...] = split((u_ref[...].astype(F32) * g_ref[...].astype(F32) * gain).astype(BF16))
    pl.semaphore_wait(barrier, n - 1)
    start_all(0, gh_rows, gh_cols)
    gh_cols[me] = gh_rows[me]

    mask = lower_mask(block)
    f_masked[...] = jnp.where(mask, f_ref[...].astype(F32), 0.0).astype(BF16)
    fm_rows[...] = split(dot(f_masked[...], x_ref[...]).astype(BF16))
    start_all(1, fm_rows, fm_cols)
    fm_cols[me] = fm_rows[me]

    nb = s_ref.shape[1]
    s_rows = lax.broadcasted_iota(jnp.int32, (block, nb), 0)
    s_lanes = lax.broadcasted_iota(jnp.int32, (block, nb), 1)
    causal = s_lanes <= s_rows // jpd
    place = (
        lax.broadcasted_iota(jnp.int32, (nb, block), 0)
        == lax.broadcasted_iota(jnp.int32, (nb, block), 1) // jpd
    )
    place = jnp.where(place, 1.0, 0.0).astype(BF16)
    same = (
        lax.broadcasted_iota(jnp.int32, (block, block), 0) % jpd
        == lax.broadcasted_iota(jnp.int32, (block, block), 1) % jpd
    )
    s_masked = jnp.where(causal, s_ref[...].astype(F32), 0.0).astype(BF16)
    weights[...] = jnp.where(same, dot(s_masked, place), 0.0).astype(BF16)

    wait_all(0, gh_rows, gh_cols)
    back_cols[...] = split(dot(weights[...], rows(gh_cols), 0, 0).astype(BF16))
    start_all(2, back_cols, back_rows)
    back_rows[me] = back_cols[me]

    wait_all(1, fm_rows, fm_cols)
    second = dot(weights[...], rows(fm_cols)).astype(BF16)
    sec_cols[...] = split(second)
    start_all(3, sec_cols, sec_rows)
    sec_rows[me] = sec_cols[me]

    products = rows(gh_cols).astype(F32) * second.astype(F32)
    gain_all[me] = jnp.sum(products.reshape(block // 8, 8, channels), axis=0)

    @pl.loop(1, n)
    def _(k):
        peer = lax.rem(me + k, n)
        copy_to(4, gain_all, gain_all, peer, me).start()

    pairs = jnp.where(same, dot(rows(gh_cols), rows(fm_cols), 1, 1), 0.0).astype(BF16)
    gsec_ref[...] = jnp.where(causal, dot(pairs, place, 1, 1), 0.0).astype(BF16)

    wait_all(2, back_cols, back_rows)
    back = rows(back_rows)
    gfirst_ref[...] = jnp.where(mask, dot(back, x_ref[...], 1, 1), 0.0).astype(BF16)
    gin_ref[...] = dot(f_masked[...], back, 0, 0).astype(BF16)

    wait_all(3, sec_cols, sec_rows)
    hidden = rows(sec_rows).astype(F32) * gain
    out_ref[...] = (g_ref[...].astype(F32) * hidden).astype(BF16)
    ggate_ref[...] = (u_ref[...].astype(F32) * hidden).astype(BF16)

    @pl.loop(1, n)
    def _(k):
        peer = lax.rem(me + k, n)
        copy_from(4, gain_all, gain_all, peer, me).wait_recv()

    total = jnp.sum(jnp.sum(gain_all[...], axis=0), axis=0, keepdims=True)
    ggain_ref[...] = total / gain * (1.0 / math.sqrt(block * n))

    @pl.loop(1, n)
    def _(k):
        peer = lax.rem(me + k, n)
        copy_to(0, gh_rows, gh_cols, peer, peer).wait_send()
        copy_to(1, fm_rows, fm_cols, peer, peer).wait_send()
        copy_to(2, back_cols, back_rows, peer, peer).wait_send()
        copy_to(3, sec_cols, sec_rows, peer, peer).wait_send()
        copy_to(4, gain_all, gain_all, peer, me).wait_send()


def fused(n, inputs, gates, cotangent, first_factor, second_factor, channel_gain):
    block, channels = inputs.shape
    jpd, nb = second_factor.shape[0], second_factor.shape[1]
    s_rows = jnp.swapaxes(second_factor, 0, 1).reshape(nb * jpd, nb)
    tokens = jax.ShapeDtypeStruct((block, channels), BF16)
    exchange = pltpu.VMEM((n, jpd, channels), BF16)
    out, gin, ggate, gfirst, gsec, ggain = pl.pallas_call(
        functools.partial(fused_kernel, n),
        out_shape=(
            tokens, tokens, tokens,
            jax.ShapeDtypeStruct((block, block), BF16),
            jax.ShapeDtypeStruct((nb * jpd, nb), BF16),
            jax.ShapeDtypeStruct((1, channels), F32),
        ),
        in_specs=[pl.BlockSpec(memory_space=pltpu.VMEM)] * 6,
        out_specs=[pl.BlockSpec(memory_space=pltpu.VMEM)] * 6,
        scratch_shapes=[
            pltpu.VMEM((block, block), BF16),
            pltpu.VMEM((block, block), BF16),
            *[exchange] * 8,
            pltpu.VMEM((n, 8, channels), F32),
            pltpu.SemaphoreType.DMA((5, n)),
            pltpu.SemaphoreType.DMA((5, n)),
        ],
        compiler_params=pltpu.CompilerParams(
            collective_id=0, has_side_effects=True, vmem_limit_bytes=48 * 1024 * 1024
        ),
    )(inputs, gates, cotangent, first_factor[0], s_rows, channel_gain[None])
    gsec = jnp.swapaxes(gsec.reshape(nb, jpd, nb), 0, 1)
    return out, gin, ggate, gfirst[None], gsec, ggain[0]


def exchanged(inputs, gates, cotangent, first_factor, second_factor, channel_gain):
    block_count, block_size = first_factor.shape[:2]
    token_rows, channels = inputs.shape
    mask_first = lower_mask(block_size)
    mask_second = lower_mask(second_factor.shape[1])
    first_masked = jnp.where(mask_first[None], first_factor, jnp.zeros((), BF16))
    second_masked = jnp.where(mask_second[None], second_factor, jnp.zeros((), BF16))
    norm_factor = 1.0 / math.sqrt(token_rows * lax.axis_size("seq"))
    by_block = lambda value: value.reshape(block_count, block_size, channels)
    rows3 = by_block(inputs)
    gates3 = by_block(gates).astype(F32)
    upstream3 = by_block(cotangent).astype(F32)
    to_cols = lambda value: lax.all_to_all(value, "seq", split_axis=1, concat_axis=0, tiled=True)
    to_rows = lambda value: lax.all_to_all(value, "seq", split_axis=0, concat_axis=1, tiled=True)
    product = functools.partial(jnp.einsum, preferred_element_type=F32)
    hidden_cols = to_cols((upstream3 * gates3 * channel_gain).astype(BF16))
    columns = to_cols(product("kab,kbc->kac", first_masked, rows3).astype(BF16))
    back_rows = to_rows(product("jab,ajc->bjc", second_masked, hidden_cols).astype(BF16))
    second_rows = to_rows(product("jab,bjc->ajc", second_masked, columns).astype(BF16)).astype(F32)
    pairs = product("ajc,bjc->jab", hidden_cols, columns)
    grad_sec = jnp.where(mask_second[None], pairs, 0.0).astype(BF16)
    pairs_first = product("kac,kbc->kab", back_rows, rows3)
    grad_first = jnp.where(mask_first[None], pairs_first, 0.0).astype(BF16)
    grad_in = product("kab,kac->kbc", first_masked, back_rows).astype(BF16)
    out = (gates3 * channel_gain * second_rows).astype(BF16)
    grad_gate = (upstream3 * channel_gain * second_rows).astype(BF16)
    gain_grad = lax.psum(jnp.sum(upstream3 * gates3 * second_rows, axis=(0, 1)), "seq") * norm_factor
    flat = lambda value: value.reshape(token_rows, channels)
    return flat(out), flat(grad_in), flat(grad_gate), grad_first, grad_sec, gain_grad


def on_device(*args):
    n = lax.axis_size("seq")
    first_factor, second_factor = args[3], args[4]
    if first_factor.shape[0] == 1 and second_factor.shape[0] % 16 == 0:
        return fused(n, *args)
    return exchanged(*args)


def solution(mesh):
    placed = (
        P(("groups", "seq"), None),
        P(("groups", "seq"), None),
        P(("groups", "seq"), None),
        P("seq", None, None),
        P("seq", None, None),
        P(),
    )
    return jax.shard_map(
        on_device,
        mesh=mesh,
        in_specs=placed,
        out_specs=(
            P(("groups", "seq"), None),
            P(("groups", "seq"), None),
            P(("groups", "seq"), None),
            P(("groups", "seq"), None, None),
            P(("groups", "seq"), None, None),
            P("groups"),
        ),
        check_vma=False,
    )
```

time: 197 us -> 94.7 us (0.48)
  Pallas kernels: 0 us -> 81.7 us
  waiting for transfers between devices: 64.6 us -> 0 us
  blocking collectives: 38.5 us -> 0 us
  starting transfers between devices: 35.1 us -> 0 us
  other arithmetic: 18.3 us -> 0.61 us
  local copies, waits for them, and re-layouts: 27.5 us -> 10.2 us
  matrix products: 11.3 us -> 0 us
    pallas_call x0 -> x1, Pallas kernels: none -> 81.7 us  [fused(): pl.pallas_call(functools.partial(fused_kernel, n), out_shape=(tokens, tok...]
    all_to_all x6 -> x0, waiting for transfers between devices: 64.6 us -> none  [the longest x1 17.7 us: on_device(): lax.all_to_all(back_cols, 'seq', split_axis=0, concat_axis=1, tiled=True)]
    psum x1 -> x0, blocking collectives: 38.5 us -> none  [on_device(): gain_grad = lax.psum(partial_gain, 'seq') * norm_factor]
    all_to_all x6 -> x0, starting transfers between devices: 35.1 us -> none  [the longest x1 7.57 us: on_device(): lax.all_to_all(first_mixed, 'seq', split_axis=1, concat_axis=0, tiled=True)]
    unnamed x3 -> x0, other arithmetic: 16.3 us -> none
    unnamed x30 -> x12, local copies, waits for them, and re-layouts: 20.3 us -> 7.87 us
    dot_general x6 -> x0, matrix products: 11.3 us -> none  [the longest x1 2.62 us: on_device(): jnp.einsum('kab,kac->kbc', first_masked, back_rows, preferred_element_typ...]
    convert_element_type x4 -> x0, local copies, waits for them, and re-layouts: 4.55 us -> none  [the longest x1 1.21 us: on_device(): first_mixed = jnp.einsum('kab,kbc->kac', first_masked, rows3, preferred_e...]
  transfers between devices with their start and end apart: 6 -> 0, of which waited for: 5 -> 0; matrix products, arithmetic and copies ran while one was open for 19% -> 0% of each run, Pallas kernels for 0% -> 0%
where the time goes in v1:
time: 94.7 us; the launch traced here: 93.2 us
  Pallas kernels  81.7 us (86%)
  local copies, waits for them, and re-layouts  10.2 us (11%)
    pallas_call x1, Pallas kernels, fused(): pl.pallas_call(functools.partial(fused_kernel, n), out_shape=(tokens, tok...  81.7 us
    unnamed x12, local copies, waits for them, and re-layouts  7.87 us

profile of v1, /device:TPU:0, one launch (start us, length us, event | category | flops | bytes accessed | tf_op | source)
XLA Modules:
  0.0 93.2 jit_solution(17036690718308644573)
XLA Ops:
  0.6 0.7 broadcast_in_dim.6.gain_ref
  1.3 1.0 %copy.12 = bf16[16,32,16]{2,1,0:T(8,128)(2,1)S(1)} copy(bf16[16,32,16]{1,2,0:T(8,128)(2,1)} %bitcast.10) | data formatting | bytes 32768 | tf_op jit(solution)/shard_map/transpose | solution.py:158
  2.3 0.0 copy-start
  2.3 1.1 %copy-done = bf16[512,768]{1,0:T(8,128)(2,1)S(1)} copy-done((bf16[512,768]{1,0:T(8,128)(2,1)S(1)}, bf16[512,768]{1,0:T(8,128)(2,1)}, u32[]{:S(2)}) %copy-start) | copy-done | bytes 786456
  3.4 0.0 copy-start.1
  3.4 1.1 %copy-done.1 = bf16[512,768]{1,0:T(8,128)(2,1)S(1)} copy-done((bf16[512,768]{1,0:T(8,128)(2,1)S(1)}, bf16[512,768]{1,0:T(8,128)(2,1)}, u32[]{:S(2)}) %copy-start.1) | copy-done | bytes 786456
  4.6 0.0 copy-start.2
  4.6 1.1 %copy-done.2 = bf16[512,768]{1,0:T(8,128)(2,1)S(1)} copy-done((bf16[512,768]{1,0:T(8,128)(2,1)S(1)}, bf16[512,768]{1,0:T(8,128)(2,1)}, u32[]{:S(2)}) %copy-start.2) | copy-done | bytes 786456
  5.7 0.0 copy-start.3
  5.7 1.0 %copy-done.3 = bf16[1,512,512]{2,1,0:T(8,128)(2,1)S(1)} copy-done((bf16[1,512,512]{2,1,0:T(8,128)(2,1)S(1)}, bf16[1,512,512]{2,1,0:T(8,128)(2,1)}, u32[]{:S(2)}) %copy-start.3) | copy-done | bytes 524312
  6.7 81.7 %shard_map.109 = (bf16[512,768]{1,0:T(8,128)(2,1)S(1)}, bf16[512,768]{1,0:T(8,128)(2,1)S(1)}, bf16[512,768]{1,0:T(8,128)(2,1)S(1)}, bf16[512,512]{1,0:T(8,128)(2...) custom-call(bf16[512,768]{1,0:T(8,128)(2,1)S(1)} %copy-done, bf16[512,768]{1,0:T(8,128)(2,1)S(1)} %copy-done.1, ...), custom_call_target="tpu_custom_call" | custom-call | tf_op jit(solution)/shard_map/pallas_call | solution.py:161
  88.4 0.6 reduce
  89.0 0.7 copy.13
  89.8 0.9 copy.18
  90.6 0.9 copy.19
  91.5 0.9 copy.20
  92.4 0.8 copy.21
Async XLA Ops:
  2.3 1.1 %copy-start = (bf16[512,768]{1,0:T(8,128)(2,1)S(1)}, bf16[512,768]{1,0:T(8,128)(2,1)}, u32[]{:S(2)}) copy-start(bf16[512,768]{1,0:T(8,128)(2,1)} %x_ref.1) | copy-start | bytes 2359300
  3.4 1.1 %copy-start.1 = (bf16[512,768]{1,0:T(8,128)(2,1)S(1)}, bf16[512,768]{1,0:T(8,128)(2,1)}, u32[]{:S(2)}) copy-start(bf16[512,768]{1,0:T(8,128)(2,1)} %g_ref.1) | copy-start | bytes 2359300
  4.6 1.1 %copy-start.2 = (bf16[512,768]{1,0:T(8,128)(2,1)S(1)}, bf16[512,768]{1,0:T(8,128)(2,1)}, u32[]{:S(2)}) copy-start(bf16[512,768]{1,0:T(8,128)(2,1)} %u_ref.1) | copy-start | bytes 2359300
  5.7 1.0 %copy-start.3 = (bf16[1,512,512]{2,1,0:T(8,128)(2,1)S(1)}, bf16[1,512,512]{2,1,0:T(8,128)(2,1)}, u32[]{:S(2)}) copy-start(bf16[1,512,512]{2,1,0:T(8,128)(2,1)} %param.9) | copy-start | bytes 1572868

commit v2 on v1

v2 whole, which is shorter than its diff:
```python
import functools
import math

import jax
import jax.numpy as jnp
from jax import lax
from jax.experimental import pallas as pl
from jax.experimental.pallas import tpu as pltpu
from jax.sharding import PartitionSpec as P

BF16 = jnp.bfloat16
F32 = jnp.float32


def lower_mask(extent):
    row_ids = lax.broadcasted_iota(jnp.int32, (extent, extent), 0)
    col_ids = lax.broadcasted_iota(jnp.int32, (extent, extent), 1)
    return col_ids <= row_ids


def dot(a, b, ca=1, cb=0):
    return lax.dot_general(a, b, (((ca,), (cb,)), ((), ())), preferred_element_type=F32)


def fused_kernel(
    n, x_ref, g_ref, u_ref, f_ref, s_ref, gain_ref,
    out_ref, gin_ref, ggate_ref, gfirst_ref, gsec_ref, ggain_ref,
    f_masked, weights, s_all, gh_rows, fm_rows, gh_cols, fm_cols, back_cols, sec_cols, back_rows, sec_rows,
    part_out, part_in, gsec_part, gsec_in, gain_all,
    flat_send, flat_recv, line_send, line_recv, part_send, part_recv, small_send, small_recv, gain_send, gain_recv,
):
    block, channels = x_ref.shape
    jpd = block // n
    side = 4
    tile = side * jpd
    me = lax.axis_index("seq")
    z, q = me // side, lax.rem(me, side)
    barrier = pltpu.get_barrier_semaphore()

    @pl.loop(1, n)
    def _(k):
        pl.semaphore_signal(
            barrier, inc=1, device_id={"seq": lax.rem(me + k, n)}, device_id_type=pl.DeviceIdType.MESH
        )

    def remote(src, dst, send, recv, peer):
        return pltpu.make_async_remote_copy(
            src_ref=src, dst_ref=dst, send_sem=send, recv_sem=recv,
            device_id={"seq": peer}, device_id_type=pl.DeviceIdType.MESH,
        )

    def flat_pair(phase, t, peer_q, slot):
        if phase == 0:
            return gh_rows.at[t, peer_q], gh_cols.at[t, z, slot]
        if phase == 1:
            return fm_rows.at[t, peer_q], fm_cols.at[t, z, slot]
        if phase == 2:
            return back_cols.at[t, peer_q], back_rows.at[t, slot]
        return sec_cols.at[t, peer_q], sec_rows.at[t, slot]

    def flat_copy(phase, t, peer_q, slot):
        src, dst = flat_pair(phase, t, peer_q, slot)
        return remote(
            src, dst, flat_send.at[phase, t, peer_q], flat_recv.at[phase, t, slot], z * side + peer_q
        )

    def flat_start(phase, t):
        @pl.loop(1, side)
        def _(k):
            peer_q = lax.rem(q + k, side)
            flat_copy(phase, t, peer_q, q).start()

    def flat_wait(phase, t):
        @pl.loop(1, side)
        def _(k):
            peer_q = lax.rem(q + k, side)
            flat_copy(phase, t, peer_q, peer_q).wait_recv()

    def line_copy(phase, t, source, target):
        cols = gh_cols if phase == 0 else fm_cols
        return remote(
            cols.at[t, source], cols.at[t, source],
            line_send.at[phase, t, target], line_recv.at[phase, t, source], target * side + q,
        )

    line_routes = {0: ((1, 0, 1), (1, 0, 2)), 1: ((1, 1, 2),), 2: ((0, 2, 1),), 3: ((0, 3, 2), (0, 3, 1))}

    def part_copy(t, target):
        return remote(part_out.at[t], part_in.at[t], part_send.at[t], part_recv.at[t], target * side + q)

    def s_copy(target, source):
        return remote(
            s_all.at[z], s_all.at[source], small_send.at[0, target], small_recv.at[0, source], target * side + q
        )

    def gsec_copy(target, source):
        return remote(
            gsec_part.at[target], gsec_in.at[source],
            small_send.at[1, target], small_recv.at[1, source], target * side + q,
        )

    def gain_copy(peer, source):
        return remote(gain_all.at[me], gain_all.at[source], gain_send.at[peer], gain_recv.at[source], peer)

    gain = gain_ref[...]
    by_piece = lambda value: value.reshape(side, side, jpd, channels)
    piece = lambda value: value.astype(BF16).reshape(side, jpd, channels)
    flat = lambda value: value.reshape(-1, channels)

    gh_rows[...] = by_piece((u_ref[...].astype(F32) * g_ref[...].astype(F32) * gain).astype(BF16))
    nb = s_ref.shape[0]
    up = lax.broadcasted_iota(jnp.int32, (nb, block), 0)
    causal = up <= lax.broadcasted_iota(jnp.int32, (nb, block), 1) // jpd
    s_all[z] = jnp.where(causal, s_ref[...].astype(F32), 0.0).astype(BF16)
    gsec_part[...] = jnp.zeros_like(gsec_part)

    pl.semaphore_wait(barrier, n - 1)
    flat_start(0, 0)

    @pl.loop(1, side)
    def _(k):
        target = lax.rem(z + k, side)
        s_copy(target, z).start()

    mask = lower_mask(block)
    f_masked[...] = jnp.where(mask, f_ref[...].astype(F32), 0.0).astype(BF16)
    fm_rows[...] = by_piece(dot(f_masked[...], x_ref[...]).astype(BF16))
    for t in range(side):
        flat_start(1, t)
        if t + 1 < side:
            flat_start(0, t + 1)
    for t in range(side):
        gh_cols[t, z, q] = gh_rows[t, q]
        fm_cols[t, z, q] = fm_rows[t, q]

    @pl.loop(1, side)
    def _(k):
        source = lax.rem(z + k, side)
        s_copy(source, source).wait_recv()

    place = (
        lax.broadcasted_iota(jnp.int32, (block, nb), 0) // jpd
        == lax.broadcasted_iota(jnp.int32, (block, nb), 1)
    )
    place = jnp.where(place, 1.0, 0.0).astype(BF16)
    same = (
        lax.broadcasted_iota(jnp.int32, (block, block), 0) % jpd
        == lax.broadcasted_iota(jnp.int32, (block, block), 1) % jpd
    )

    @pl.loop(0, side)
    def _(t):
        flat_wait(0, t)
        flat_wait(1, t)
        for role, routes in line_routes.items():
            @pl.when(z == role)
            def _():
                for phase, source, target in routes:
                    line_copy(phase, t, source, target).start()
        weights[t] = jnp.where(same, dot(place, s_all[t]), 0.0).astype(BF16)

    def add_pairs(t, low, high, first, last):
        rows, lanes = (high - low) * tile, (last - first) * tile
        own = (
            lax.broadcasted_iota(jnp.int32, (rows, lanes), 0) % jpd
            == lax.broadcasted_iota(jnp.int32, (rows, lanes), 1) % jpd
        )
        pairs = dot(flat(fm_cols[t, low:high]), flat(gh_cols[t, first:last]), 1, 1)
        pairs = jnp.where(own, pairs, 0.0).astype(BF16)
        sums = dot(place[low * tile:high * tile], pairs, 0, 0).astype(BF16)
        gsec_part[t, :, first * tile:last * tile] = gsec_part[t, :, first * tile:last * tile] + sums

    def send_second(t, second, plane):
        sec_cols[t] = piece(second)
        flat_start(3, t)
        products = second.astype(BF16).astype(F32) * flat(gh_cols[t, plane]).astype(F32)
        sums = jnp.sum(products.reshape(tile // 8, 8, channels), axis=0)
        gain_all[me] = jnp.where(t == 0, 0.0, gain_all[me]) + sums

    def send_back(t, back):
        back_cols[t] = piece(back)
        flat_start(2, t)

    w = lambda t, low, high, first, last: weights[t, low * tile:high * tile, first * tile:last * tile]

    gain_all[me] = jnp.zeros((8, channels), F32)

    @pl.when(z == 0)
    def _():
        @pl.loop(0, side)
        def _(t):
            send_second(t, dot(w(t, 0, 1, 0, 1), flat(fm_cols[t, 0:1]), 0, 0), 0)
            add_pairs(t, 0, 1, 0, 1)

        @pl.loop(0, side)
        def _(t):
            back = dot(w(t, 0, 1, 0, 1), flat(gh_cols[t, 0:1]))
            part_copy(t, 0).wait_recv()
            send_back(t, back + flat(part_in[t]).astype(F32))

    @pl.when(z == 3)
    def _():
        @pl.loop(0, side)
        def _(t):
            send_back(t, dot(w(t, 3, 4, 3, 4), flat(gh_cols[t, 3:4])))
            add_pairs(t, 3, 4, 3, 4)

        @pl.loop(0, side)
        def _(t):
            second = dot(w(t, 3, 4, 3, 4), flat(fm_cols[t, 3:4]), 0, 0)
            part_copy(t, 3).wait_recv()
            send_second(t, second + flat(part_in[t]).astype(F32), 3)

    @pl.when(z == 1)
    def _():
        @pl.loop(0, side)
        def _(t):
            line_copy(0, t, 2, 1).wait_recv()
            line_copy(0, t, 3, 1).wait_recv()
            both = dot(w(t, 0, 2, 1, 4), flat(gh_cols[t, 1:4]))
            part_out[t] = piece(both[:tile])
            part_copy(t, 0).start()
            send_back(t, both[tile:])
            line_copy(1, t, 0, 1).wait_recv()
            send_second(t, dot(w(t, 0, 2, 1, 2), flat(fm_cols[t, 0:2]), 0, 0), 1)
            add_pairs(t, 0, 2, 1, 3)

    @pl.when(z == 2)
    def _():
        @pl.loop(0, side)
        def _(t):
            line_copy(1, t, 0, 2).wait_recv()
            line_copy(1, t, 1, 2).wait_recv()
            both = dot(w(t, 0, 3, 2, 4), flat(fm_cols[t, 0:3]), 0, 0)
            part_out[t] = piece(both[tile:])
            part_copy(t, 3).start()
            send_second(t, both[:tile], 2)
            line_copy(0, t, 3, 2).wait_recv()
            send_back(t, dot(w(t, 2, 3, 2, 4), flat(gh_cols[t, 2:4])))
            add_pairs(t, 0, 3, 3, 4)
            add_pairs(t, 2, 3, 2, 3)

    @pl.loop(1, n)
    def _(k):
        gain_copy(lax.rem(me + k, n), me).start()

    @pl.loop(1, side)
    def _(k):
        gsec_copy(lax.rem(z + k, side), z).start()

    for t in range(side):
        back_rows[t, q] = back_cols[t, q]
        sec_rows[t, q] = sec_cols[t, q]
    for t in range(side):
        rows = slice(t * tile, (t + 1) * tile)
        flat_wait(3, t)
        hidden = flat(sec_rows[t]).astype(F32) * gain
        out_ref[rows] = (g_ref[rows].astype(F32) * hidden).astype(BF16)
        ggate_ref[rows] = (u_ref[rows].astype(F32) * hidden).astype(BF16)
        flat_wait(2, t)
        first = dot(flat(back_rows[t]), x_ref[...], 1, 1)
        gfirst_ref[rows] = jnp.where(mask[rows], first, 0.0).astype(BF16)
    gin_ref[...] = dot(f_masked[...], flat(back_rows[...]), 0, 0).astype(BF16)

    gsec_in[z] = gsec_part[z]

    @pl.loop(1, side)
    def _(k):
        source = lax.rem(z + k, side)
        gsec_copy(source, source).wait_recv()

    gsec_sum = jnp.sum(gsec_in[...].astype(F32), axis=0)
    gsec_ref[...] = jnp.where(causal, gsec_sum, 0.0).astype(BF16)

    @pl.loop(1, n)
    def _(k):
        peer = lax.rem(me + k, n)
        gain_copy(peer, peer).wait_recv()

    total = jnp.sum(jnp.sum(gain_all[...], axis=0), axis=0, keepdims=True)
    ggain_ref[...] = total / gain * (1.0 / math.sqrt(block * n))

    @pl.loop(0, side)
    def _(t):
        @pl.loop(1, side)
        def _(k):
            peer_q = lax.rem(q + k, side)
            for phase in range(4):
                flat_copy(phase, t, peer_q, q).wait_send()
        for role, routes in line_routes.items():
            @pl.when(z == role)
            def _():
                for phase, source, target in routes:
                    line_copy(phase, t, source, target).wait_send()
                if role in (1, 2):
                    part_copy(t, 0 if role == 1 else 3).wait_send()

    @pl.loop(1, side)
    def _(k):
        target = lax.rem(z + k, side)
        s_copy(target, z).wait_send()
        gsec_copy(target, z).wait_send()

    @pl.loop(1, n)
    def _(k):
        gain_copy(lax.rem(me + k, n), me).wait_send()


def fused(n, inputs, gates, cotangent, first_factor, second_factor, channel_gain):
    block, channels = inputs.shape
    jpd, nb = second_factor.shape[0], second_factor.shape[1]
    side = 4
    s_lanes = jnp.transpose(second_factor, (2, 1, 0)).reshape(nb, nb * jpd)
    tokens = jax.ShapeDtypeStruct((block, channels), BF16)
    pieces = pltpu.VMEM((side, side, jpd, channels), BF16)
    planes = pltpu.VMEM((side, side, side, jpd, channels), BF16)
    small = pltpu.VMEM((side, nb, block), BF16)
    dma = pltpu.SemaphoreType.DMA
    out, gin, ggate, gfirst, gsec, ggain = pl.pallas_call(
        functools.partial(fused_kernel, n),
        out_shape=(
            tokens, tokens, tokens,
            jax.ShapeDtypeStruct((block, block), BF16),
            jax.ShapeDtypeStruct((nb, block), BF16),
            jax.ShapeDtypeStruct((1, channels), F32),
        ),
        in_specs=[pl.BlockSpec(memory_space=pltpu.VMEM)] * 6,
        out_specs=[pl.BlockSpec(memory_space=pltpu.VMEM)] * 6,
        scratch_shapes=[
            pltpu.VMEM((block, block), BF16),
            pltpu.VMEM((side, block, block), BF16),
            small,
            pieces, pieces, planes, planes, pieces, pieces, pieces, pieces, pieces, pieces,
            small, small,
            pltpu.VMEM((n, 8, channels), F32),
            dma((4, side, side)), dma((4, side, side)),
            dma((2, side, side)), dma((2, side, side)),
            dma((side,)), dma((side,)),
            dma((2, side)), dma((2, side)),
            dma((n,)), dma((n,)),
        ],
        compiler_params=pltpu.CompilerParams(
            collective_id=0, has_side_effects=True, vmem_limit_bytes=48 * 1024 * 1024
        ),
    )(inputs, gates, cotangent, first_factor[0], s_lanes, channel_gain[None])
    gsec = jnp.transpose(gsec.reshape(nb, nb, jpd), (2, 1, 0))
    return out, gin, ggate, gfirst[None], gsec, ggain[0]


def exchanged(inputs, gates, cotangent, first_factor, second_factor, channel_gain):
    block_count, block_size = first_factor.shape[:2]
    token_rows, channels = inputs.shape
    mask_first = lower_mask(block_size)
    mask_second = lower_mask(second_factor.shape[1])
    first_masked = jnp.where(mask_first[None], first_factor, jnp.zeros((), BF16))
    second_masked = jnp.where(mask_second[None], second_factor, jnp.zeros((), BF16))
    norm_factor = 1.0 / math.sqrt(token_rows * lax.axis_size("seq"))
    by_block = lambda value: value.reshape(block_count, block_size, channels)
    rows3 = by_block(inputs)
    gates3 = by_block(gates).astype(F32)
    upstream3 = by_block(cotangent).astype(F32)
    to_cols = lambda value: lax.all_to_all(value, "seq", split_axis=1, concat_axis=0, tiled=True)
    to_rows = lambda value: lax.all_to_all(value, "seq", split_axis=0, concat_axis=1, tiled=True)
    product = functools.partial(jnp.einsum, preferred_element_type=F32)
    hidden_cols = to_cols((upstream3 * gates3 * channel_gain).astype(BF16))
    columns = to_cols(product("kab,kbc->kac", first_masked, rows3).astype(BF16))
    back_rows = to_rows(product("jab,ajc->bjc", second_masked, hidden_cols).astype(BF16))
    second_rows = to_rows(product("jab,bjc->ajc", second_masked, columns).astype(BF16)).astype(F32)
    pairs = product("ajc,bjc->jab", hidden_cols, columns)
    grad_sec = jnp.where(mask_second[None], pairs, 0.0).astype(BF16)
    pairs_first = product("kac,kbc->kab", back_rows, rows3)
    grad_first = jnp.where(mask_first[None], pairs_first, 0.0).astype(BF16)
    grad_in = product("kab,kac->kbc", first_masked, back_rows).astype(BF16)
    out = (gates3 * channel_gain * second_rows).astype(BF16)
    grad_gate = (upstream3 * channel_gain * second_rows).astype(BF16)
    gain_grad = lax.psum(jnp.sum(upstream3 * gates3 * second_rows, axis=(0, 1)), "seq") * norm_factor
    flat = lambda value: value.reshape(token_rows, channels)
    return flat(out), flat(grad_in), flat(grad_gate), grad_first, grad_sec, gain_grad


def on_device(*args):
    n = lax.axis_size("seq")
    first_factor, second_factor = args[3], args[4]
    if n == 16 and first_factor.shape[0] == 1 and second_factor.shape[0] % 16 == 0:
        return fused(n, *args)
    return exchanged(*args)


def solution(mesh):
    placed = (
        P(("groups", "seq"), None),
        P(("groups", "seq"), None),
        P(("groups", "seq"), None),
        P("seq", None, None),
        P("seq", None, None),
        P(),
    )
    return jax.shard_map(
        on_device,
        mesh=mesh,
        in_specs=placed,
        out_specs=(
            P(("groups", "seq"), None),
            P(("groups", "seq"), None),
            P(("groups", "seq"), None),
            P(("groups", "seq"), None, None),
            P(("groups", "seq"), None, None),
            P("groups"),
        ),
        check_vma=False,
    )
```

time: 94.7 us -> 81.4 us (0.86); the launches traced: 93.2 us -> 81 us
  Pallas kernels: 81.7 us -> 69.6 us
    pallas_call x1, Pallas kernels: 81.7 us -> 69.6 us  [fused(): pl.pallas_call(functools.partial(fused_kernel, n), out_shape=(tokens, tok...]
    unnamed x12 -> x14, local copies, waits for them, and re-layouts: 7.87 us -> 8.43 us
where the time goes in v2:
time: 81.4 us; the launch traced here: 81 us
  Pallas kernels  69.6 us (86%)
  local copies, waits for them, and re-layouts  10.2 us (13%)
    pallas_call x1, Pallas kernels, fused(): pl.pallas_call(functools.partial(fused_kernel, n), out_shape=(tokens, tok...  69.6 us
    unnamed x14, local copies, waits for them, and re-layouts  8.43 us

profile of v2, /device:TPU:0, one launch (start us, length us, event | category | flops | bytes accessed | tf_op | source)
XLA Modules:
  0.0 81.0 jit_solution(4233190104623107945)
XLA Ops:
  0.6 0.9 %copy.12 = bf16[16,16,32]{2,1,0:T(8,128)(2,1)S(1)} copy(bf16[16,16,32]{2,0,1:T(8,128)(2,1)} %bitcast.8) | data formatting | bytes 32768 | tf_op jit(solution)/shard_map/transpose | solution.py:313
  1.5 0.0 copy-start.4
  1.5 0.1 reshape.18.s_ref
  1.6 0.6 copy-done.4
  2.2 0.0 copy-start
  2.2 1.1 %copy-done = bf16[512,768]{1,0:T(8,128)(2,1)S(1)} copy-done((bf16[512,768]{1,0:T(8,128)(2,1)S(1)}, bf16[512,768]{1,0:T(8,128)(2,1)}, u32[]{:S(2)}) %copy-start) | copy-done | bytes 786456
  3.3 0.0 copy-start.1
  3.3 1.1 %copy-done.1 = bf16[512,768]{1,0:T(8,128)(2,1)S(1)} copy-done((bf16[512,768]{1,0:T(8,128)(2,1)S(1)}, bf16[512,768]{1,0:T(8,128)(2,1)}, u32[]{:S(2)}) %copy-start.1) | copy-done | bytes 786456
  4.5 0.0 copy-start.2
  4.5 1.1 %copy-done.2 = bf16[512,768]{1,0:T(8,128)(2,1)S(1)} copy-done((bf16[512,768]{1,0:T(8,128)(2,1)S(1)}, bf16[512,768]{1,0:T(8,128)(2,1)}, u32[]{:S(2)}) %copy-start.2) | copy-done | bytes 786456
  5.6 0.0 copy-start.3
  5.6 1.0 %copy-done.3 = bf16[1,512,512]{2,1,0:T(8,128)(2,1)S(1)} copy-done((bf16[1,512,512]{2,1,0:T(8,128)(2,1)S(1)}, bf16[1,512,512]{2,1,0:T(8,128)(2,1)}, u32[]{:S(2)}) %copy-start.3) | copy-done | bytes 524312
  6.6 69.6 %shard_map.109 = (bf16[512,768]{1,0:T(8,128)(2,1)S(1)}, bf16[512,768]{1,0:T(8,128)(2,1)S(1)}, bf16[512,768]{1,0:T(8,128)(2,1)S(1)}, bf16[512,512]{1,0:T(8,128)(2...) custom-call(bf16[512,768]{1,0:T(8,128)(2,1)S(1)} %copy-done, bf16[512,768]{1,0:T(8,128)(2,1)S(1)} %copy-done.1, ...), custom_call_target="tpu_custom_call" | custom-call | tf_op jit(solution)/shard_map/pallas_call | solution.py:319
  76.2 0.1 reshape.19
  76.4 0.6 copy.15
  77.0 0.6 reduce
  77.6 0.9 %copy.20 = bf16[512,768]{1,0:T(8,128)(2,1)} copy(bf16[512,768]{1,0:T(8,128)(2,1)S(1)} %get-tuple-element.24) | data formatting | bytes 1572864
  78.5 0.9 %copy.21 = bf16[512,768]{1,0:T(8,128)(2,1)} copy(bf16[512,768]{1,0:T(8,128)(2,1)S(1)} %get-tuple-element.25) | data formatting | bytes 1572864
  79.4 0.9 %copy.22 = bf16[512,768]{1,0:T(8,128)(2,1)} copy(bf16[512,768]{1,0:T(8,128)(2,1)S(1)} %get-tuple-element.26) | data formatting | bytes 1572864
  80.2 0.8 copy.23
  (1 shorter events, 0.0 us)
Async XLA Ops:
  1.5 0.7 copy-start.4
  2.2 1.1 %copy-start = (bf16[512,768]{1,0:T(8,128)(2,1)S(1)}, bf16[512,768]{1,0:T(8,128)(2,1)}, u32[]{:S(2)}) copy-start(bf16[512,768]{1,0:T(8,128)(2,1)} %x_ref.1) | copy-start | bytes 2359300
  3.3 1.1 %copy-start.1 = (bf16[512,768]{1,0:T(8,128)(2,1)S(1)}, bf16[512,768]{1,0:T(8,128)(2,1)}, u32[]{:S(2)}) copy-start(bf16[512,768]{1,0:T(8,128)(2,1)} %g_ref.1) | copy-start | bytes 2359300
  4.5 1.1 %copy-start.2 = (bf16[512,768]{1,0:T(8,128)(2,1)S(1)}, bf16[512,768]{1,0:T(8,128)(2,1)}, u32[]{:S(2)}) copy-start(bf16[512,768]{1,0:T(8,128)(2,1)} %u_ref.1) | copy-start | bytes 2359300
  5.6 1.0 %copy-start.3 = (bf16[1,512,512]{2,1,0:T(8,128)(2,1)S(1)}, bf16[1,512,512]{2,1,0:T(8,128)(2,1)}, u32[]{:S(2)}) copy-start(bf16[1,512,512]{2,1,0:T(8,128)(2,1)} %param.9) | copy-start | bytes 1572868

commit v3 on v2

--- a/solution.py
+++ b/solution.py
@@ -23,11 +23,11 @@
 
 
 def fused_kernel(
-    n, x_ref, g_ref, u_ref, f_ref, s_ref, gain_ref,
+    n, x_hbm, g_hbm, u_hbm, f_hbm, s_ref, gain_ref,
     out_ref, gin_ref, ggate_ref, gfirst_ref, gsec_ref, ggain_ref,
-    f_masked, weights, s_all, gh_rows, fm_rows, gh_cols, fm_cols, back_cols, sec_cols, back_rows, sec_rows,
-    part_out, part_in, gsec_part, gsec_in, gain_all,
-    flat_send, flat_recv, line_send, line_recv, part_send, part_recv, small_send, small_recv, gain_send, gain_recv,
+    x_ref, g_ref, u_ref, f_ref, gin_acc, f_masked, weights, s_all, gh_rows, fm_rows, gh_cols, fm_cols, back_cols, sec_cols, back_rows, sec_rows,
+    part_out, part_in, gsec_part, gsec_in, gain_part, gain_all,
+    flat_send, flat_recv, line_send, line_recv, part_send, part_recv, small_send, small_recv, gain_send, gain_recv, load,
 ):
     block, channels = x_ref.shape
     jpd = block // n
@@ -35,6 +35,12 @@
     tile = side * jpd
     me = lax.axis_index("seq")
     z, q = me // side, lax.rem(me, side)
+    loads = [
+        pltpu.make_async_copy(src, dst, load.at[k])
+        for k, (src, dst) in enumerate(((f_hbm, f_ref), (x_hbm, x_ref), (g_hbm, g_ref), (u_hbm, u_ref)))
+    ]
+    for copy in loads:
+        copy.start()
     barrier = pltpu.get_barrier_semaphore()
 
     @pl.loop(1, n)
@@ -83,7 +89,7 @@
             line_send.at[phase, t, target], line_recv.at[phase, t, source], target * side + q,
         )
 
-    line_routes = {0: ((1, 0, 1), (1, 0, 2)), 1: ((1, 1, 2),), 2: ((0, 2, 1),), 3: ((0, 3, 2), (0, 3, 1))}
+    line_routes = {0: ((1, 0, 2), (1, 0, 1)), 1: ((1, 1, 2),), 2: ((0, 2, 1),), 3: ((0, 3, 1), (0, 3, 2))}
 
     def part_copy(t, target):
         return remote(part_out.at[t], part_in.at[t], part_send.at[t], part_recv.at[t], target * side + q)
@@ -107,28 +113,48 @@
     piece = lambda value: value.astype(BF16).reshape(side, jpd, channels)
     flat = lambda value: value.reshape(-1, channels)
 
-    gh_rows[...] = by_piece((u_ref[...].astype(F32) * g_ref[...].astype(F32) * gain).astype(BF16))
     nb = s_ref.shape[0]
     up = lax.broadcasted_iota(jnp.int32, (nb, block), 0)
     causal = up <= lax.broadcasted_iota(jnp.int32, (nb, block), 1) // jpd
     s_all[z] = jnp.where(causal, s_ref[...].astype(F32), 0.0).astype(BF16)
     gsec_part[...] = jnp.zeros_like(gsec_part)
 
+    for copy in loads:
+        copy.wait()
     pl.semaphore_wait(barrier, n - 1)
-    flat_start(0, 0)
 
     @pl.loop(1, side)
     def _(k):
         target = lax.rem(z + k, side)
         s_copy(target, z).start()
 
-    mask = lower_mask(block)
-    f_masked[...] = jnp.where(mask, f_ref[...].astype(F32), 0.0).astype(BF16)
-    fm_rows[...] = by_piece(dot(f_masked[...], x_ref[...]).astype(BF16))
-    for t in range(side):
-        flat_start(1, t)
-        if t + 1 < side:
-            flat_start(0, t + 1)
+    def strip_mask(t):
+        ids = lambda dim: lax.broadcasted_iota(jnp.int32, (tile, block), dim)
+        return ids(1) <= ids(0) + t * tile
+
+    def send_hidden():
+        for t in range(side):
+            rows = slice(t * tile, (t + 1) * tile)
+            gh_rows[t] = piece(u_ref[rows].astype(F32) * g_ref[rows].astype(F32) * gain)
+            flat_start(0, t)
+
+    def send_mixed():
+        for t in range(side):
+            rows, depth = slice(t * tile, (t + 1) * tile), (t + 1) * tile
+            f_masked[rows] = jnp.where(strip_mask(t), f_ref[rows].astype(F32), 0.0).astype(BF16)
+            fm_rows[t] = piece(dot(f_masked[rows, :depth], x_ref[:depth]))
+            flat_start(1, t)
+
+    @pl.when(z < 2)
+    def _():
+        send_mixed()
+        send_hidden()
+
+    @pl.when(z >= 2)
+    def _():
+        send_hidden()
+        send_mixed()
+
     for t in range(side):
         gh_cols[t, z, q] = gh_rows[t, q]
         fm_cols[t, z, q] = fm_rows[t, q]
@@ -144,20 +170,24 @@
     )
     place = jnp.where(place, 1.0, 0.0).astype(BF16)
     same = (
-        lax.broadcasted_iota(jnp.int32, (block, block), 0) % jpd
-        == lax.broadcasted_iota(jnp.int32, (block, block), 1) % jpd
+        lax.broadcasted_iota(jnp.int32, (tile, block), 0) % jpd
+        == lax.broadcasted_iota(jnp.int32, (tile, block), 1) % jpd
     )
+    strips = {0: (0,), 1: (0, 1), 2: (0, 1, 2), 3: (3,)}
 
     @pl.loop(0, side)
     def _(t):
-        flat_wait(0, t)
-        flat_wait(1, t)
         for role, routes in line_routes.items():
             @pl.when(z == role)
             def _():
+                for phase in ((1, 0) if role < 2 else (0, 1)):
+                    if any(route[0] == phase for route in routes):
+                        flat_wait(phase, t)
                 for phase, source, target in routes:
                     line_copy(phase, t, source, target).start()
-        weights[t] = jnp.where(same, dot(place, s_all[t]), 0.0).astype(BF16)
+                for a in strips[role]:
+                    rows = slice(a * tile, (a + 1) * tile)
+                    weights[t, rows] = jnp.where(same, dot(place[rows], s_all[t]), 0.0).astype(BF16)
 
     def add_pairs(t, low, high, first, last):
         rows, lanes = (high - low) * tile, (last - first) * tile
@@ -174,8 +204,7 @@
         sec_cols[t] = piece(second)
         flat_start(3, t)
         products = second.astype(BF16).astype(F32) * flat(gh_cols[t, plane]).astype(F32)
-        sums = jnp.sum(products.reshape(tile // 8, 8, channels), axis=0)
-        gain_all[me] = jnp.where(t == 0, 0.0, gain_all[me]) + sums
+        gain_part[...] = gain_part[...] + jnp.sum(products.reshape(tile // 8, 8, channels), axis=0)
 
     def send_back(t, back):
         back_cols[t] = piece(back)
@@ -183,12 +212,13 @@
 
     w = lambda t, low, high, first, last: weights[t, low * tile:high * tile, first * tile:last * tile]
 
-    gain_all[me] = jnp.zeros((8, channels), F32)
+    gain_part[...] = jnp.zeros_like(gain_part)
 
     @pl.when(z == 0)
     def _():
         @pl.loop(0, side)
         def _(t):
+            flat_wait(0, t)
             send_second(t, dot(w(t, 0, 1, 0, 1), flat(fm_cols[t, 0:1]), 0, 0), 0)
             add_pairs(t, 0, 1, 0, 1)
 
@@ -202,6 +232,7 @@
     def _():
         @pl.loop(0, side)
         def _(t):
+            flat_wait(1, t)
             send_back(t, dot(w(t, 3, 4, 3, 4), flat(gh_cols[t, 3:4])))
             add_pairs(t, 3, 4, 3, 4)
 
@@ -215,6 +246,7 @@
     def _():
         @pl.loop(0, side)
         def _(t):
+            flat_wait(0, t)
             line_copy(0, t, 2, 1).wait_recv()
             line_copy(0, t, 3, 1).wait_recv()
             both = dot(w(t, 0, 2, 1, 4), flat(gh_cols[t, 1:4]))
@@ -229,6 +261,7 @@
     def _():
         @pl.loop(0, side)
         def _(t):
+            flat_wait(1, t)
             line_copy(1, t, 0, 2).wait_recv()
             line_copy(1, t, 1, 2).wait_recv()
             both = dot(w(t, 0, 3, 2, 4), flat(fm_cols[t, 0:3]), 0, 0)
@@ -240,6 +273,8 @@
             add_pairs(t, 0, 3, 3, 4)
             add_pairs(t, 2, 3, 2, 3)
 
+    gain_all[me] = jnp.sum(gain_part[...], axis=0, keepdims=True)
+
     @pl.loop(1, n)
     def _(k):
         gain_copy(lax.rem(me + k, n), me).start()
@@ -251,6 +286,7 @@
     for t in range(side):
         back_rows[t, q] = back_cols[t, q]
         sec_rows[t, q] = sec_cols[t, q]
+    last = block - tile
     for t in range(side):
         rows = slice(t * tile, (t + 1) * tile)
         flat_wait(3, t)
@@ -259,8 +295,12 @@
         ggate_ref[rows] = (u_ref[rows].astype(F32) * hidden).astype(BF16)
         flat_wait(2, t)
         first = dot(flat(back_rows[t]), x_ref[...], 1, 1)
-        gfirst_ref[rows] = jnp.where(mask[rows], first, 0.0).astype(BF16)
-    gin_ref[...] = dot(f_masked[...], flat(back_rows[...]), 0, 0).astype(BF16)
+        gfirst_ref[rows] = jnp.where(strip_mask(t), first, 0.0).astype(BF16)
+        if t == side - 2:
+            gin_acc[:last] = dot(f_masked[:last, :last], flat(back_rows[:side - 1]), 0, 0)
+    final = dot(f_masked[last:], flat(back_rows[side - 1]), 0, 0)
+    gin_ref[:last] = (gin_acc[:last] + final[:last]).astype(BF16)
+    gin_ref[last:] = final[last:].astype(BF16)
 
     gsec_in[z] = gsec_part[z]
 
@@ -277,7 +317,7 @@
         peer = lax.rem(me + k, n)
         gain_copy(peer, peer).wait_recv()
 
-    total = jnp.sum(jnp.sum(gain_all[...], axis=0), axis=0, keepdims=True)
+    total = jnp.sum(gain_all[...], axis=0)
     ggain_ref[...] = total / gain * (1.0 / math.sqrt(block * n))
 
     @pl.loop(0, side)
@@ -324,20 +364,24 @@
             jax.ShapeDtypeStruct((nb, block), BF16),
             jax.ShapeDtypeStruct((1, channels), F32),
         ),
-        in_specs=[pl.BlockSpec(memory_space=pltpu.VMEM)] * 6,
+        in_specs=[pl.BlockSpec(memory_space=pltpu.HBM)] * 4 + [pl.BlockSpec(memory_space=pltpu.VMEM)] * 2,
         out_specs=[pl.BlockSpec(memory_space=pltpu.VMEM)] * 6,
         scratch_shapes=[
+            *[pltpu.VMEM((block, channels), BF16)] * 3,
+            pltpu.VMEM((block, block), BF16),
+            pltpu.VMEM((block, channels), F32),
             pltpu.VMEM((block, block), BF16),
             pltpu.VMEM((side, block, block), BF16),
             small,
             pieces, pieces, planes, planes, pieces, pieces, pieces, pieces, pieces, pieces,
             small, small,
-            pltpu.VMEM((n, 8, channels), F32),
+            pltpu.VMEM((8, channels), F32),
+            pltpu.VMEM((n, 1, channels), F32),
             dma((4, side, side)), dma((4, side, side)),
             dma((2, side, side)), dma((2, side, side)),
             dma((side,)), dma((side,)),
             dma((2, side)), dma((2, side)),
-            dma((n,)), dma((n,)),
+            dma((n,)), dma((n,)), dma((4,)),
         ],
         compiler_params=pltpu.CompilerParams(
             collective_id=0, has_side_effects=True, vmem_limit_bytes=48 * 1024 * 1024

time: 81.4 us -> 72 us (0.88)
  Pallas kernels: 69.6 us -> 60.2 us
    pallas_call x1, Pallas kernels: 69.6 us -> 60.2 us  [fused(): pl.pallas_call(functools.partial(fused_kernel, n), out_shape=(tokens, tok...]
where the time goes in v3:
time: 72 us; the launch traced here: 71.6 us
  Pallas kernels  60.2 us (84%)
  local copies, waits for them, and re-layouts  10.2 us (14%)
    pallas_call x1, Pallas kernels, fused(): pl.pallas_call(functools.partial(fused_kernel, n), out_shape=(tokens, tok...  60.2 us
    unnamed x14, local copies, waits for them, and re-layouts  8.43 us

profile of v3, /device:TPU:0, one launch (start us, length us, event | category | flops | bytes accessed | tf_op | source)
XLA Modules:
  0.0 71.6 jit_solution(508603173006095543)
XLA Ops:
  0.6 0.9 %copy.12 = bf16[16,16,32]{2,1,0:T(8,128)(2,1)S(1)} copy(bf16[16,16,32]{2,0,1:T(8,128)(2,1)} %bitcast.8) | data formatting | bytes 32768 | tf_op jit(solution)/shard_map/transpose | solution.py:353
  1.5 0.0 copy-start.4
  1.5 0.1 reshape.18.s_ref
  1.6 0.6 copy-done.4
  2.2 0.0 copy-start
  2.2 1.1 %copy-done = bf16[512,768]{1,0:T(8,128)(2,1)S(1)} copy-done((bf16[512,768]{1,0:T(8,128)(2,1)S(1)}, bf16[512,768]{1,0:T(8,128)(2,1)}, u32[]{:S(2)}) %copy-start) | copy-done | bytes 786456
  3.3 0.0 copy-start.1
  3.3 1.1 %copy-done.1 = bf16[512,768]{1,0:T(8,128)(2,1)S(1)} copy-done((bf16[512,768]{1,0:T(8,128)(2,1)S(1)}, bf16[512,768]{1,0:T(8,128)(2,1)}, u32[]{:S(2)}) %copy-start.1) | copy-done | bytes 786456
  4.5 0.0 copy-start.2
  4.5 1.1 %copy-done.2 = bf16[512,768]{1,0:T(8,128)(2,1)S(1)} copy-done((bf16[512,768]{1,0:T(8,128)(2,1)S(1)}, bf16[512,768]{1,0:T(8,128)(2,1)}, u32[]{:S(2)}) %copy-start.2) | copy-done | bytes 786456
  5.6 0.0 copy-start.3
  5.6 1.0 %copy-done.3 = bf16[1,512,512]{2,1,0:T(8,128)(2,1)S(1)} copy-done((bf16[1,512,512]{2,1,0:T(8,128)(2,1)S(1)}, bf16[1,512,512]{2,1,0:T(8,128)(2,1)}, u32[]{:S(2)}) %copy-start.3) | copy-done | bytes 524312
  6.6 60.2 %shard_map.109 = (bf16[512,768]{1,0:T(8,128)(2,1)S(1)}, bf16[512,768]{1,0:T(8,128)(2,1)S(1)}, bf16[512,768]{1,0:T(8,128)(2,1)S(1)}, bf16[512,512]{1,0:T(8,128)(2...) custom-call(bf16[512,768]{1,0:T(8,128)(2,1)S(1)} %copy-done, bf16[512,768]{1,0:T(8,128)(2,1)S(1)} %copy-done.1, ...), custom_call_target="tpu_custom_call" | custom-call | tf_op jit(solution)/shard_map/pallas_call | solution.py:359
  66.8 0.1 reshape.19
  67.0 0.6 copy.15
  67.6 0.6 reduce
  68.2 0.9 %copy.20 = bf16[512,768]{1,0:T(8,128)(2,1)} copy(bf16[512,768]{1,0:T(8,128)(2,1)S(1)} %get-tuple-element.24) | data formatting | bytes 1572864
  69.1 0.9 %copy.21 = bf16[512,768]{1,0:T(8,128)(2,1)} copy(bf16[512,768]{1,0:T(8,128)(2,1)S(1)} %get-tuple-element.25) | data formatting | bytes 1572864
  70.0 0.9 %copy.22 = bf16[512,768]{1,0:T(8,128)(2,1)} copy(bf16[512,768]{1,0:T(8,128)(2,1)S(1)} %get-tuple-element.26) | data formatting | bytes 1572864
  70.8 0.8 %copy.23 = bf16[1,512,512]{2,1,0:T(8,128)(2,1)} copy(bf16[1,512,512]{2,1,0:T(8,128)(2,1)S(1)} %bitcast.6) | data formatting | bytes 1048576
  (1 shorter events, 0.0 us)
Async XLA Ops:
  1.5 0.7 copy-start.4
  2.2 1.1 %copy-start = (bf16[512,768]{1,0:T(8,128)(2,1)S(1)}, bf16[512,768]{1,0:T(8,128)(2,1)}, u32[]{:S(2)}) copy-start(bf16[512,768]{1,0:T(8,128)(2,1)} %x_hbm.1) | copy-start | bytes 2359300
  3.3 1.1 %copy-start.1 = (bf16[512,768]{1,0:T(8,128)(2,1)S(1)}, bf16[512,768]{1,0:T(8,128)(2,1)}, u32[]{:S(2)}) copy-start(bf16[512,768]{1,0:T(8,128)(2,1)} %g_hbm.1) | copy-start | bytes 2359300
  4.5 1.1 %copy-start.2 = (bf16[512,768]{1,0:T(8,128)(2,1)S(1)}, bf16[512,768]{1,0:T(8,128)(2,1)}, u32[]{:S(2)}) copy-start(bf16[512,768]{1,0:T(8,128)(2,1)} %u_hbm.1) | copy-start | bytes 2359300
  5.6 1.0 %copy-start.3 = (bf16[1,512,512]{2,1,0:T(8,128)(2,1)S(1)}, bf16[1,512,512]{2,1,0:T(8,128)(2,1)}, u32[]{:S(2)}) copy-start(bf16[1,512,512]{2,1,0:T(8,128)(2,1)} %param.9) | copy-start | bytes 1572868
